TPU v7x, 256 devices: a whole 4x4x8 slice. The times are simulated.
256 devices in a mesh: grp: 16 (over y_hi, z), head: 16 (over x, y_lo, core).
Axes of the slice: x: 4, y: 4 (y_hi: 2, y_lo: 2; y = y_hi * 2 + y_lo), z: 8, core: 2. Of those that a mesh axis runs over, the one named last changes fastest.
Arguments:
- q_latent: bfloat16 [1024, 1536], P(('grp', 'head')), may hold values from -6 to 6
- draft_latent: bfloat16 [1024, 512], P(('grp', 'head')), may hold values from -6 to 6
- draft_rope: bfloat16 [1024, 64], P(('grp', 'head')), may hold values from -6 to 6
- draft_start: int32 [128], P('grp'), may hold values from 0 to 7
- prompt_latent: bfloat16 [8192, 512], P(('grp', 'head')), may hold values from -100 to 100
- prompt_rope: bfloat16 [8192, 64], P(('grp', 'head')), may hold values from -6 to 6
- w_uq: bfloat16 [1536, 24576], P(None, 'head'), may hold values from -0.15625 to 0.15625
- w_uk: bfloat16 [128, 128, 512], P('head'), may hold values from -0.5 to 0.5
- w_uv: bfloat16 [128, 512, 128], P('head'), may hold values from -0.25 to 0.25
Outputs:
- attn_out: bfloat16 [1024, 16384], P('grp', 'head')
All inputs are finite; a program needn't handle non-finite values.
Results may differ from a plain program's by a relative error of at most 0.01.
The roundings to bfloat16 on the way count: a program that leaves them out, or rounds other values in their place, can miss the bound.
Values may be sent and summed in bfloat16 or wider, within the bound.
A program may use at most 64 MiB of HBM per device.

v0:
```python
import math

import jax
import jax.numpy as jnp
from jax import lax
from jax.sharding import PartitionSpec as P

KVL = 512
ROPE = 64
NOPE = 128
VD = 128
DRAFT = 8
PROMPT = 8192


def rotate(rope_q, positions):
    half = ROPE // 2
    freq = 10000.0 ** (-jnp.arange(half, dtype=jnp.float32) / half)
    angle = positions[:, None].astype(jnp.float32) * freq[None, :]
    cosine = jnp.cos(angle)[:, None, :]
    sine = jnp.sin(angle)[:, None, :]
    values = rope_q.astype(jnp.float32)
    first = values[..., :half]
    second = values[..., half:]
    return jnp.concatenate(
        [first * cosine - second * sine, second * cosine + first * sine], axis=-1
    ).astype(jnp.bfloat16)


def draft_bias(starts, count):
    rows = jnp.arange(count, dtype=jnp.int32)
    same = rows[:, None] // DRAFT == rows[None, :] // DRAFT
    key_start = jnp.repeat(starts, DRAFT)
    upper = rows[None, :] % DRAFT <= rows[:, None] % DRAFT
    lower = key_start[None, :] <= rows[None, :] % DRAFT
    return jnp.where(same & upper & lower, 0.0, -1e30).astype(jnp.float32)


def absorb(state, q_abs, q_rot, latent, rope, bias):
    top, total, summed = state
    scale = 1.0 / (NOPE + ROPE) ** 0.5
    scores = (
        jnp.dot(q_abs, latent.T, preferred_element_type=jnp.float32)
        + jnp.dot(q_rot, rope.T, preferred_element_type=jnp.float32)
    ) * scale
    scores = scores + bias
    new_top = jnp.maximum(top, jnp.max(scores, axis=1))
    factor = jnp.exp(top - new_top)
    expd = jnp.exp(scores - new_top[:, None])
    total = total * factor + jnp.sum(expd, axis=1)
    summed = summed * factor[:, None] + jnp.dot(
        expd.astype(jnp.bfloat16), latent, preferred_element_type=jnp.float32
    )
    return (new_top, total, summed)


def absorb_blocks(state, q_abs, q_rot, latent, rope):
    rows = latent.shape[0]
    block = math.gcd(rows, 2048)
    count = rows // block
    lat_blocks = latent.reshape(count, block, latent.shape[1])
    rope_blocks = rope.reshape(count, block, rope.shape[1])

    def step(carry, pieces):
        return (absorb(carry, q_abs, q_rot, pieces[0], pieces[1], 0.0), None)

    result, unused = lax.scan(step, state, (lat_blocks, rope_blocks))
    return result


def on_device(
    q_latent, draft_latent, draft_rope, draft_start, prompt_latent, prompt_rope, w_uq, w_uk, w_uv
):
    q_rows, d_lat, d_rope = (
        lax.all_gather(q_latent, "head", axis=0, tiled=True),
        lax.all_gather(draft_latent, "head", axis=0, tiled=True),
        lax.all_gather(draft_rope, "head", axis=0, tiled=True),
    )
    count = q_rows.shape[0]
    heads = w_uk.shape[0]
    q_full = jnp.dot(q_rows, w_uq, preferred_element_type=jnp.float32).astype(jnp.bfloat16)
    q_full = q_full.reshape(count, heads, NOPE + ROPE)
    positions = PROMPT + jnp.arange(count, dtype=jnp.int32) % DRAFT
    q_rot = rotate(q_full[..., NOPE:], positions).reshape(count * heads, ROPE)
    q_abs = jnp.einsum(
        "rhd,hdc->rhc", q_full[..., :NOPE], w_uk, preferred_element_type=jnp.float32
    ).astype(jnp.bfloat16)
    q_abs = q_abs.reshape(count * heads, KVL)
    queries = count * heads
    initial = (
        jnp.full((queries,), -1e30, jnp.float32),
        jnp.zeros((queries,), jnp.float32),
        jnp.zeros((queries, KVL), jnp.float32),
    )
    full_lat, full_rope = (
        lax.all_gather(prompt_latent, ("grp", "head"), axis=0, tiled=True),
        lax.all_gather(prompt_rope, ("grp", "head"), axis=0, tiled=True),
    )
    state = absorb_blocks(initial, q_abs, q_rot, full_lat, full_rope)
    bias = jnp.broadcast_to(
        draft_bias(draft_start, count)[:, None, :], (count, heads, count)
    ).reshape(queries, count)
    top, total, summed = absorb(state, q_abs, q_rot, d_lat, d_rope, bias)
    context = (summed / total[:, None]).astype(jnp.bfloat16).reshape(count, heads, KVL)
    output = jnp.einsum("rhc,hcv->rhv", context, w_uv, preferred_element_type=jnp.float32).astype(
        jnp.bfloat16
    )
    return output.reshape(count, heads * VD)


def solution(mesh):
    in_specs = (
        P(("grp", "head"), None),
        P(("grp", "head"), None),
        P(("grp", "head"), None),
        P("grp"),
        P(("grp", "head"), None),
        P(("grp", "head"), None),
        P(None, "head"),
        P("head", None, None),
        P("head", None, None),
    )
    out_specs = P("grp", "head")
    return jax.shard_map(
        on_device, mesh=mesh, in_specs=in_specs, out_specs=out_specs, check_vma=False
    )
```

profile of v0, /device:TPU:1, one launch (start us, length us, event | category | flops | bytes accessed | tf_op | source)
XLA Modules:
  0.0 900.4 jit_solution(15023704450931655130)
XLA Ops:
  6.5 0.7 all-gather.8.cloned.1.call-update
  7.3 0.0 all-gather.6.cloned.1.call-start
  7.3 0.7 all-gather.6.cloned.1.call-update
  8.0 21.8 %all-gather = bf16[16,4,1536]{2,1,0:T(4,128)(2,1)S(1)} all-gather(bf16[1,4,1536]{2,1,0:T(4,128)(2,1)} %bitcast.64), channel_id=1, replica_groups=mesh['grp'=16,'head'=16] {'head'}, dimensions={0}, use_global_device_ids=true | all-gather | bytes 208896 | tf_op jit(solution)/shard_map/all_gather | solution.py:75
  29.8 0.1 reshape.269
  29.9 0.0 copy-start.4
  29.9 3.3 convolution_convert_fusion
  33.2 0.2 reshape.262
  33.4 0.1 broadcast_in_dim.23
  33.5 0.1 broadcast_in_dim_reshape.3
  33.6 0.1 and_select_fusion
  33.7 0.1 copy.19
  33.9 16.4 %all-gather.1 = bf16[16,4,512]{2,1,0:T(4,128)(2,1)S(1)} all-gather(bf16[1,4,512]{2,1,0:T(4,128)(2,1)S(1)} %bitcast.65), channel_id=1, replica_groups=mesh['grp'=16,'head'=16] {'head'}, dimensions={0}, use_global_device_ids=true | all-gather | bytes 69632 | tf_op jit(solution)/shard_map/all_gather | solution.py:76
  50.3 0.3 fusion.24
  50.6 1.1 copy.33
  51.7 17.6 %all-gather.2 = bf16[16,4,64]{2,1,0:T(4,128)(2,1)S(1)} all-gather(bf16[1,4,64]{2,1,0:T(4,128)(2,1)S(1)} %bitcast.66), channel_id=1, replica_groups=mesh['grp'=16,'head'=16] {'head'}, dimensions={0}, use_global_device_ids=true | all-gather | bytes 8704 | tf_op jit(solution)/shard_map/all_gather | solution.py:77
  69.3 0.2 multiply_cosine_fusion
  69.5 0.2 fusion.29
  69.7 0.1 pad_maximum_fusion
  69.8 0.2 fusion.39
  70.0 0.4 fusion.38
  70.4 349.4 %all-gather.8.cloned.1.call-done = bf16[8192,64]{1,0:T(8,128)(2,1)} async-done(((bf16[32,64]{1,0:T(8,128)(2,1)}), bf16[8192,64]{1,0:T(8,128)(2,1)}) %all-gather.8.cloned.1.call-update) | async-done | bytes 1048592 | tf_op jit(solution)/shard_map/all_gather | solution.py:97
  419.8 419.2 %all-gather.6.cloned.1.call-done = bf16[8192,512]{1,0:T(8,128)(2,1)} async-done(((bf16[32,512]{1,0:T(8,128)(2,1)}), bf16[8192,512]{1,0:T(8,128)(2,1)}) %all-gather.6.cloned.1.call-update) | async-done | bytes 8388624 | tf_op jit(solution)/shard_map/all_gather | solution.py:96
  839.0 52.3 %while.15 = (s32[]{:T(128)}, f32[512]{0:T(512)S(1)}, f32[512]{0:T(512)S(1)}, f32[512,512]{1,0:T(8,128)S(1)}, bf16[4,2048,512]{2,1,0:T(8,128)(2,1)}, /*index=5*/b...) while((s32[]{:T(128)}, f32[512]{0:T(512)S(1)}, ...), condition=%wide.region_3.4_spmd.clone, body=%wide.region_0.3_spmd.clone.sunk | while | flops 2289830400 | bytes 45188748 | solution.py:67
  839.0 3.0 fusion.65
  842.0 3.7 fusion.66
  845.7 3.0 fusion.67
  848.7 0.5 copy-done.1
  849.1 2.9 fusion.69
  852.1 3.0 fusion.65
  855.0 3.7 fusion.66
  858.8 3.0 fusion.67
  861.8 0.5 copy-done.1
  862.2 2.9 fusion.69
  865.2 3.0 fusion.65
  868.1 3.7 fusion.66
  871.9 3.0 fusion.67
  874.8 0.5 copy-done.1
  875.3 2.9 fusion.69
  878.2 3.0 fusion.65
  881.2 3.7 fusion.66
  884.9 3.0 fusion.67
  887.9 0.5 copy-done.1
  888.4 2.9 fusion.69
  891.4 0.4 fusion.23
  891.8 0.8 copy-done.2
  892.5 0.4 fusion.27
  892.9 0.7 copy.34
  (39 shorter events, 0.3 us)
Async XLA Ops:
  6.5 43.8 %copy-start = (bf16[8,128,512]{2,1,0:T(8,128)(2,1)S(1)}, bf16[8,128,512]{2,1,0:T(8,128)(2,1)}, u32[]{:S(2)}) copy-start(bf16[8,128,512]{2,1,0:T(8,128)(2,1)} %param.18) | copy-start | bytes 3145732
  6.5 26.9 %copy-start.5 = (s32[8]{0:T(128)S(1)}, s32[8]{0:T(128)}, u32[]{:S(2)}) copy-start(s32[8]{0:T(128)} %param.14) | copy-start | bytes 100
  6.5 27.3 %copy-start.3 = (bf16[4,512]{1,0:T(4,128)(2,1)S(1)}, bf16[4,512]{1,0:T(4,128)(2,1)}, u32[]{:S(2)}) copy-start(bf16[4,512]{1,0:T(4,128)(2,1)} %param.12) | copy-start | bytes 12292
  6.5 413.2 %all-gather.8.cloned.1.call-start = ((), (), s32[]{:S(2)}) async-start(), calls=%async_computation.1 | async-start | bytes 2105344 | tf_op jit(solution)/shard_map/all_gather | solution.py:97
  7.3 831.7 %all-gather.6.cloned.1.call-start = ((), (), s32[]{:S(2)}) async-start(), calls=%async_computation | async-start | bytes 8421376 | tf_op jit(solution)/shard_map/all_gather | solution.py:96
  29.9 21.8 %copy-start.4 = (bf16[4,64]{1,0:T(4,128)(2,1)S(1)}, bf16[4,64]{1,0:T(4,128)(2,1)}, u32[]{:S(2)}) copy-start(bf16[4,64]{1,0:T(4,128)(2,1)} %param.13) | copy-start | bytes 1540
  845.7 3.4 copy-start.1
  858.8 3.4 copy-start.1
  871.8 3.4 copy-start.1
  884.9 3.4 copy-start.1
  891.3 1.2 copy-start.2
Sparse Core Ops, SparseCore 0:
  9.3 410.4 all-gather.7
  421.7 417.2 all-gather.5
where the time goes:
time: 901 us; the launch traced here: 900 us
  waiting for transfers between devices  770 us (85%)
  blocking collectives  55.8 us (6%)
  matrix products  43.3 us (5%)
  between operations  13.6 us (2%)
  other arithmetic  12.6 us (1%)
    all_gather x1, waiting for transfers between devices, on_device(): lax.all_gather(prompt_latent, ('grp', 'head'), axis=0, tiled=True)  419 us
    all_gather x1, waiting for transfers between devices, on_device(): lax.all_gather(prompt_rope, ('grp', 'head'), axis=0, tiled=True)  349 us
    all_gather x1, blocking collectives, on_device(): lax.all_gather(q_latent, 'head', axis=0, tiled=True)  21.8 us
  transfers between devices with their start and end apart: 2, of which 2 were waited for; matrix products, arithmetic and copies ran while one was open for 1% of the time, Pallas kernels for 0%

commit v1 on v0

v1 whole, which is shorter than its diff:
```python
import math

import jax
import jax.numpy as jnp
import numpy as np
from jax import lax
from jax.experimental import pallas as pl
from jax.experimental.pallas import tpu as pltpu
from jax.sharding import PartitionSpec as P

MESH = pl.DeviceIdType.MESH
KVL = 512
ROPE = 64
NOPE = 128
VD = 128
DRAFT = 8
PROMPT = 8192
QLORA = 1536
ROWS = 64
HEADS = 8
GROUP = ROWS * HEADS
SCALE = math.log2(math.e) / math.sqrt(NOPE + ROPE)
UNIT = 9
UNITS = 128
BLOCK = 256
NT = (((1,), (1,)), ((), ()))


def rotation_table():
    half = ROPE // 2
    freq = np.float32(10000.0) ** (-np.arange(half, dtype=np.float32) / np.float32(half))
    position = PROMPT + np.arange(DRAFT, dtype=np.float32)
    angle = (position[:, None] * freq[None, :].astype(np.float32)).astype(np.float64)
    zero = np.zeros((DRAFT, 2 * half))
    cosine = np.concatenate([np.cos(angle), np.cos(angle), zero], axis=1)
    sine = np.concatenate([-np.sin(angle), np.sin(angle), zero], axis=1)
    return np.concatenate([cosine, sine], axis=0).astype(np.float32)


def early(bs, cs, as_):
    return (bs * 2 + cs) * 4 + as_


def late(bs, cs, as_, zs=0):
    return 32 + ((bs * 2 + cs) * 4 + as_) * 3 + zs


def chunks():
    both = (0, 1)
    first = [early(b, c, a) for c in both for b in range(3) for a in range(4)]
    first += [early(3, c, 0) for c in both] + [late(0, c, 0, z) for c in both for z in range(3)]
    second = [late(b, c, a, z) for c in both for b, a in ((0, 1), (0, 2), (0, 3), (1, 0), (2, 0)) for z in range(3)]
    second += [early(3, c, 3) for c in both]
    third = [late(b, c, 1, z) for c in both for b in (1, 2) for z in range(3)]
    third += [late(b, c, 2, z) for c in both for b in (1, 2) for z in range(3)]
    fourth = [late(b, c, 3, z) for c in both for b in (1, 2) for z in range(3)]
    fourth += [late(3, c, 0, z) for c in both for z in range(3)]
    fourth += [early(3, c, a) for c in both for a in (1, 2)] + [late(3, c, 1, 0) for c in both]
    fifth = [late(3, c, 1, z) for c in both for z in (1, 2)]
    fifth += [late(3, c, a, z) for c in both for a in (2, 3) for z in range(3)]
    return first, second, third, fourth, fifth


def dot_t(a, b):
    return lax.dot_general(a, b, NT, preferred_element_type=jnp.float32)


def dot(a, b):
    return jnp.dot(a, b, preferred_element_type=jnp.float32)


def kernel(
    ql_ref, dl_ref, dr_ref, start_ref, pl_ref, pr_ref, table_ref, w_uq, w_uk, w_uv, out_ref,
    keys, q_send, q_all, q_stage, q_own, q_peer, q_full, queries, draft, acc, top, total,
    o_send, o_recv, s_send, s_recv, v_uq, v_uk, v_uv, local_sem, send_sem, recv_sem,
):
    grp, head = lax.axis_index("grp"), lax.axis_index("head")
    x, y, z, core = head // 4, (grp // 8) * 2 + (head // 2) % 2, grp % 8, head % 2
    toward = 2 * (z % 2) - 1

    def place(px, py, pz, pc):
        return ((py // 2) * 8 + pz, px * 4 + (py % 2) * 2 + pc)

    def at_a(step):
        return place((x + step * core + 4) % 4, (y + step * (1 - core) + 4) % 4, z, core)

    def at_b(step):
        return place((x + step * (1 - core) + 4) % 4, (y + step * core + 4) % 4, z, core)

    def at_z(step):
        return place(x, y, (z + step + 8) % 8, core)

    beside = y + 1 - 2 * (y % 2)
    sibling = place(x, y, z, 1 - core)
    partner = at_z(-toward)
    q_peers = [place((x + dx) % 4, y, z, core) for dx in (1, 3, 2)]
    q_peers += [place((x + dx) % 4, beside, z, core) for dx in (0, 1, 3, 2)]
    greeted = q_peers + [place(x, (y + 3 + 2 * (y % 2)) % 4, z, core), place(x, (y + 2) % 4, z, core)]
    greeted += [at_z(toward), at_z(3 * toward), at_z(2), at_z(-2), partner, sibling]

    weights = [
        pltpu.make_async_copy(src, dst, local_sem.at[i])
        for i, (src, dst) in enumerate(((w_uq, v_uq), (w_uk, v_uk), (w_uv, v_uv)))
    ]
    for copy in weights:
        copy.start()
    barrier = pltpu.get_barrier_semaphore()
    for device in greeted:
        pl.semaphore_signal(barrier, inc=1, device_id=device, device_id_type=MESH)

    sent = []

    def send(src, dst, device):
        i = len(sent)
        copy = pltpu.make_async_remote_copy(
            src_ref=src, dst_ref=dst, send_sem=send_sem.at[i], recv_sem=recv_sem.at[i],
            device_id=device, device_id_type=MESH,
        )
        copy.start()
        sent.append(copy)
        return copy

    def tiles(unit, count=1, first=0, last=0):
        return keys.at[pl.ds(unit * UNIT + first, count * UNIT - first - last)]

    def move(src, dst, count, device, first=0, last=0):
        return send(tiles(src, count, first, last), tiles(dst, count, first, last), device)

    for row in range(2):
        for lane in range(4):
            keys[early(0, 0, 0) * UNIT + row * 4 + lane] = pl_ref[row * 16 : row * 16 + 16, lane * 128 : lane * 128 + 128]
    keys[early(0, 0, 0) * UNIT + 8] = jnp.concatenate([pr_ref[0:16, :], pr_ref[16:32, :]], axis=1)
    q_stage[...] = jnp.zeros(q_stage.shape, jnp.float32)
    for part in range(4):
        q_stage[part * 4 : part * 4 + 4, 0:384] = ql_ref[:, part * 384 : part * 384 + 384].astype(jnp.float32)
        q_stage[part * 4 : part * 4 + 4, 384:512] = dl_ref[:, part * 128 : part * 128 + 128].astype(jnp.float32)
    q_stage[0:4, 512:576] = dr_ref[...].astype(jnp.float32)
    q_send[...] = q_stage[...].astype(jnp.bfloat16)
    my_rows = pl.ds(pl.multiple_of((core * 8 + head // 2) * 16, 16), 16)
    q_all[my_rows, :] = q_send[...]

    pl.semaphore_wait(barrier, len(greeted))

    q_copies = [send(q_send, q_all.at[my_rows, :], device) for device in q_peers]
    z_copies = [
        move(early(0, 0, 0), late(0, 0, 0, slot), 1, at_z(step))
        for slot, step in enumerate((toward, -2 * toward, 3 * toward))
    ]

    class Stream:
        def __init__(self, unit, count):
            self.unit, self.count = unit, count
            self.right, self.left, self.far = [None] * 4, [None] * 4, [None] * 8
            self.side = []

        def start(self):
            unit, count = self.unit, self.count
            own = unit(0, 0, 0)
            self.a = [move(own, unit(0, 0, slot), count, at_a(step)) for slot, step in ((1, 1), (2, -1), (3, 2))]
            self.spread(0)
            self.to_sibling(0, 0, 1)

        def spread(self, k):
            unit, count = self.unit, self.count
            self.right[k] = move(unit(0, 0, k), unit(1, 0, k), count, at_b(1))
            self.left[k] = move(unit(0, 0, k), unit(2, 0, k), count, at_b(-1))

        def to_sibling(self, bs, k, width):
            unit, count = self.unit, self.count
            self.side.append(move(unit(bs, 0, k), unit(bs, 1, k), count * width, sibling))

        def arrive_a(self):
            for k in (1, 2, 3):
                self.a[k - 1].wait_recv()
                self.spread(k)
            self.to_sibling(0, 1, 3)

        def arrive_b(self, ks):
            unit, count = self.unit, self.count
            cut = count * UNIT // 2
            for k in ks:
                self.right[k].wait_recv()
                self.far[2 * k] = move(unit(1, 0, k), unit(3, 0, k), count, at_b(1), 0, count * UNIT - cut)
                self.left[k].wait_recv()
                self.far[2 * k + 1] = move(unit(2, 0, k), unit(3, 0, k), count, at_b(-1), cut, 0)
            self.to_sibling(1, ks[0], len(ks))
            self.to_sibling(2, ks[0], len(ks))

        def arrive_far(self, ks):
            for k in ks:
                self.far[2 * k].wait_recv()
                self.far[2 * k + 1].wait_recv()
            self.to_sibling(3, ks[0], len(ks))

        def arrive_sibling(self, count):
            for _ in range(count):
                self.side.pop(0).wait_recv()

    soon, later = Stream(early, 1), Stream(late, 3)
    soon.start()

    soon.arrive_a()
    for copy in z_copies:
        copy.wait_recv()
    later.start()
    for copy in q_copies:
        copy.wait_recv()
    half = pl.ds(pl.multiple_of(core * 128, 128), 128)
    q_side = send(q_all.at[half, :], q_all.at[half, :], sibling)
    soon.arrive_b([0])
    q_side.wait_recv()

    row_at = lax.broadcasted_iota(jnp.int32, (ROWS, 256), 0)
    col_at = lax.broadcasted_iota(jnp.int32, (ROWS, 256), 1)
    from_head = row_at // 4
    source = ((from_head % 2) * 8 + from_head // 2) * 16 + row_at % 4
    for part in range(4):
        pick = jnp.where(col_at == source + part * 4, 1.0, 0.0).astype(jnp.bfloat16)
        picked = dot(pick, q_all[...]).astype(jnp.bfloat16)
        q_own[:, part * 384 : part * 384 + 384] = picked[:, 0:384]
        draft[:, 128 + part * 128 : 256 + part * 128] = picked[:, 384:512]
        if part == 0:
            draft[:, 0:128] = picked[:, 512:640]
    q_peer_copy = send(q_own, q_peer, partner)

    lane = lax.broadcasted_iota(jnp.int32, (ROWS, 128), 1)

    def project(group, rows_ref):
        q_full[...] = dot(rows_ref[...], v_uq[...]).astype(jnp.bfloat16).astype(jnp.float32)
        cosine = jnp.concatenate([table_ref[0:8, :]] * 8, axis=0)
        sine = jnp.concatenate([table_ref[8:16, :]] * 8, axis=0)

        def absorb(h, nope, pe):
            rows = pl.ds(group * GROUP + h * ROWS, ROWS)
            turned = jnp.where(lane < 32, pltpu.roll(pe, 96, 1), pltpu.roll(pe, 32, 1))
            rotated = pe * cosine + turned * sine
            queries[rows, 0:128] = rotated.astype(jnp.bfloat16)
            queries[rows, 640:768] = pltpu.roll(rotated, 64, 1).astype(jnp.bfloat16)
            queries[rows, 128:640] = dot(nope.astype(jnp.bfloat16), v_uk[h]).astype(jnp.bfloat16)

        for pair in range(HEADS // 2):
            at = pair * 384
            middle = q_full[:, at + 128 : at + 256]
            end = pltpu.roll(q_full[:, at + 256 : at + 384], 64, 1)
            absorb(2 * pair, q_full[:, at : at + 128], middle)
            absorb(2 * pair + 1, jnp.where(lane < 64, pltpu.roll(middle, 64, 1), end), end)

    def score(rows, units):
        first, second = [], []
        low = [jnp.concatenate([keys[u * UNIT + t] for u in units], axis=0) for t in range(4)]
        high = [jnp.concatenate([keys[u * UNIT + 4 + t] for u in units], axis=0) for t in range(4)]
        rope = jnp.concatenate([keys[u * UNIT + 8] for u in units], axis=0)
        left = dot_t(queries[rows, 0:640], jnp.concatenate([rope] + low, axis=1))
        right = dot_t(queries[rows, 128:768], jnp.concatenate(high + [rope], axis=1))
        values = jnp.concatenate([jnp.concatenate(low, axis=1), jnp.concatenate(high, axis=1)], axis=0)
        return jnp.concatenate([left, right], axis=1) * SCALE, values

    def update(rows, scores, values, first=False):
        peak = jnp.max(scores, axis=1, keepdims=True)
        if first:
            new_top = jnp.broadcast_to(peak, (BLOCK, 128))
        else:
            old_top = top[rows, :]
            new_top = jnp.maximum(old_top, peak)
            factor = jnp.exp2(old_top - new_top)
        e = jnp.exp2(scores - new_top[:, 0:1])
        part = jnp.sum(e, axis=1, keepdims=True)
        summed = dot(e.astype(jnp.bfloat16), values)
        if first:
            total[rows, :] = jnp.broadcast_to(part, (BLOCK, 128))
            acc[rows, :] = summed
        else:
            total[rows, :] = total[rows, :] * factor + part
            acc[rows, :] = acc[rows, :] * factor[:, 0:1] + summed
        top[rows, :] = new_top

    def attend(items):
        held = None
        for group, block, units, first in items:
            rows = pl.ds(group * GROUP + block * BLOCK, BLOCK)
            now = (rows, *score(rows, units), first)
            if held is not None:
                update(*held)
            held = now
        update(*held)

    def attend_draft():
        row = lax.broadcasted_iota(jnp.int32, (BLOCK, ROWS), 0) % ROWS
        col = lax.broadcasted_iota(jnp.int32, (BLOCK, ROWS), 1)
        begin = jnp.zeros((BLOCK, ROWS), jnp.int32)
        for i in range(8):
            begin = jnp.where(col // DRAFT == i, start_ref[i], begin)
        seen = (row // DRAFT == col // DRAFT) & (col % DRAFT <= row % DRAFT) & (begin <= col % DRAFT)
        bias = jnp.where(seen, 0.0, -1e30)
        for block in range(2):
            rows = pl.ds(block * BLOCK, BLOCK)
            scores = dot_t(queries[rows, 0:640], draft[...]) * SCALE + bias
            update(rows, scores, draft[:, 128:640], True)

    def context(group, h):
        rows = pl.ds(group * GROUP + h * ROWS, ROWS)
        ctx = (acc[rows, :] * (1.0 / total[rows, 0:1])).astype(jnp.bfloat16)
        return dot(ctx, v_uv[h]), top[rows, :] + jnp.log2(total[rows, :])

    c0, c1, c2, c3, c4 = chunks()
    weights[0].wait()
    weights[1].wait()
    project(0, q_own)
    soon.arrive_b([1, 2, 3])
    attend_draft()
    soon.arrive_far([0])
    later.arrive_a()
    later.arrive_b([0])
    soon.arrive_far([1, 2, 3])
    soon.arrive_sibling(8)
    later.arrive_sibling(1)
    attend([(0, 0, c0, False), (0, 1, c0, False)])
    later.arrive_b([1])
    q_peer_copy.wait_recv()
    project(1, q_peer)
    later.arrive_b([2])
    later.arrive_sibling(3)
    attend([(0, 0, c1, False), (0, 1, c1, False)])
    later.arrive_b([3])
    later.arrive_far([0])
    attend([(1, 0, c0, True), (1, 1, c0, True), (1, 0, c1, False), (1, 1, c1, False)])
    later.arrive_far([1])
    later.arrive_sibling(4)
    attend([(1, 0, c2, False), (1, 1, c2, False)])
    later.arrive_far([2, 3])
    later.arrive_sibling(4)
    attend([(1, 0, c3, False), (1, 1, c3, False)])
    later.arrive_sibling(1)
    attend([(1, 0, c4, False), (1, 1, c4, False)])
    weights[2].wait()
    shares = jnp.zeros((ROWS, 128), jnp.float32)
    for h in range(HEADS):
        value, share = context(1, h)
        o_send[:, h * VD : h * VD + VD] = value.astype(jnp.bfloat16)
        shares = jnp.where(lane == h, share, shares)
    s_send[...] = shares
    o_copy = send(o_send, o_recv, partner)
    s_copy = send(s_send, s_recv, partner)
    attend([(0, b, c, False) for c in (c2, c3, c4) for b in range(2)])
    own = [context(0, h) for h in range(HEADS)]
    o_copy.wait_recv()
    s_copy.wait_recv()
    for h, (value, share) in enumerate(own):
        other = jnp.broadcast_to(s_recv[:, h : h + 1], (ROWS, 128))
        mine = 1.0 / (1.0 + jnp.exp2(jnp.minimum(other - share, 120.0)))
        theirs = 1.0 / (1.0 + jnp.exp2(jnp.minimum(share - other, 120.0)))
        peer = o_recv[:, h * VD : h * VD + VD].astype(jnp.float32)
        out_ref[:, h * VD : h * VD + VD] = (value * mine + peer * theirs).astype(jnp.bfloat16)
    for copy in sent:
        copy.wait_send()


def on_device(
    q_latent, draft_latent, draft_rope, draft_start, prompt_latent, prompt_rope, w_uq, w_uk, w_uv
):
    vmem = pl.BlockSpec(memory_space=pltpu.VMEM)
    smem = pl.BlockSpec(memory_space=pltpu.SMEM)
    hbm = pl.BlockSpec(memory_space=pl.ANY)
    bf16, f32 = jnp.bfloat16, jnp.float32
    return pl.pallas_call(
        kernel,
        name="attention",
        out_shape=jax.ShapeDtypeStruct((ROWS, HEADS * VD), bf16),
        in_specs=[vmem, vmem, vmem, smem, vmem, vmem, vmem, hbm, hbm, hbm],
        out_specs=vmem,
        scratch_shapes=[
            pltpu.VMEM((UNITS * UNIT, 16, 128), bf16),
            pltpu.VMEM((16, 640), bf16),
            pltpu.VMEM((256, 640), bf16),
            pltpu.VMEM((16, 640), f32),
            pltpu.VMEM((ROWS, QLORA), bf16),
            pltpu.VMEM((ROWS, QLORA), bf16),
            pltpu.VMEM((ROWS, QLORA), f32),
            pltpu.VMEM((2 * GROUP, 768), bf16),
            pltpu.VMEM((ROWS, 640), bf16),
            pltpu.VMEM((2 * GROUP, KVL), f32),
            pltpu.VMEM((2 * GROUP, 128), f32),
            pltpu.VMEM((2 * GROUP, 128), f32),
            pltpu.VMEM((ROWS, HEADS * VD), bf16),
            pltpu.VMEM((ROWS, HEADS * VD), bf16),
            pltpu.VMEM((ROWS, 128), f32),
            pltpu.VMEM((ROWS, 128), f32),
            pltpu.VMEM((QLORA, HEADS * (NOPE + ROPE)), bf16),
            pltpu.VMEM((HEADS, NOPE, KVL), bf16),
            pltpu.VMEM((HEADS, KVL, VD), bf16),
            pltpu.SemaphoreType.DMA((3,)),
            pltpu.SemaphoreType.DMA((80,)),
            pltpu.SemaphoreType.DMA((80,)),
        ],
        compiler_params=pltpu.CompilerParams(
            collective_id=0, has_side_effects=True, vmem_limit_bytes=48 * 2**20
        ),
    )(
        q_latent, draft_latent, draft_rope, draft_start, prompt_latent, prompt_rope,
        rotation_table(), w_uq, w_uk, w_uv,
    )


def solution(mesh):
    in_specs = (
        P(("grp", "head"), None),
        P(("grp", "head"), None),
        P(("grp", "head"), None),
        P("grp"),
        P(("grp", "head"), None),
        P(("grp", "head"), None),
        P(None, "head"),
        P("head", None, None),
        P("head", None, None),
    )
    out_specs = P("grp", "head")
    return jax.shard_map(
        on_device, mesh=mesh, in_specs=in_specs, out_specs=out_specs, check_vma=False
    )
```

time: 901 us -> 53.1 us (0.06)
  waiting for transfers between devices: 770 us -> 0 us
  blocking collectives: 55.8 us -> 0 us
  Pallas kernels: 0 us -> 44.7 us
  matrix products: 43.3 us -> 0 us
  between operations: 13.6 us -> 0.02 us
  other arithmetic: 12.6 us -> 0 us
    all_gather x2 -> x0, waiting for transfers between devices: 769 us -> none  [the longest x1 419 us: on_device(): lax.all_gather(prompt_latent, ('grp', 'head'), axis=0, tiled=True)]
    all_gather x3 -> x0, blocking collectives: 55.8 us -> none  [the longest x1 21.8 us: on_device(): lax.all_gather(q_latent, 'head', axis=0, tiled=True)]
    pallas_call x0 -> x1, Pallas kernels: none -> 44.7 us  [on_device(): pl.pallas_call(kernel, name='attention', out_shape=jax.ShapeDtypeStruct((...]
    dot_general x18 -> x0, matrix products: 43.3 us -> none  [the longest x5 15.1 us: absorb(): jnp.dot(q_rot, rope.T, preferred_element_type=jnp.float32)]
    reduce_sum x5 -> x0, other arithmetic: 11.9 us -> none  [absorb(): total = total * factor + jnp.sum(expd, axis=1)]
  transfers between devices with their start and end apart: 2 -> 0, of which waited for: 2 -> 0; matrix products, arithmetic and copies ran while one was open for 1% -> 0% of each run, Pallas kernels for 0% -> 0%
where the time goes in v1:
time: 53.1 us; the launch traced here: 52.7 us
  Pallas kernels  44.7 us (84%)
  local copies, waits for them, and re-layouts  7.98 us (15%)
    pallas_call x1, Pallas kernels, on_device(): pl.pallas_call(kernel, name='attention', out_shape=jax.ShapeDtypeStruct((...  44.7 us
    unnamed x19, local copies, waits for them, and re-layouts  7.98 us

profile of v1, /device:TPU:1, one launch (start us, length us, event | category | flops | bytes accessed | tf_op | source)
XLA Modules:
  0.0 52.7 jit_solution(12189668990809457031)
XLA Ops:
  0.0 0.0 copy-start
  0.0 1.2 %copy-done = bf16[8,128,512]{2,1,0:T(8,128)(2,1)S(1)} copy-done((bf16[8,128,512]{2,1,0:T(8,128)(2,1)S(1)}, bf16[8,128,512]{2,1,0:T(8,128)(2,1)}, u32[]{:S(2)}) %copy-start) | copy-done | bytes 1048600
  1.2 0.0 copy-start.1
  1.2 1.2 %copy-done.1 = bf16[8,512,128]{2,1,0:T(8,128)(2,1)S(1)} copy-done((bf16[8,512,128]{2,1,0:T(8,128)(2,1)S(1)}, bf16[8,512,128]{2,1,0:T(8,128)(2,1)}, u32[]{:S(2)}) %copy-start.1) | copy-done | bytes 1048600
  2.5 0.0 copy-start.2
  2.5 0.8 %copy-done.2 = bf16[32,512]{1,0:T(8,128)(2,1)S(1)} copy-done((bf16[32,512]{1,0:T(8,128)(2,1)S(1)}, bf16[32,512]{1,0:T(8,128)(2,1)}, u32[]{:S(2)}) %copy-start.2) | copy-done | bytes 32792
  3.2 0.0 copy-start.3
  3.2 0.7 %copy-done.3 = bf16[4,1536]{1,0:T(4,128)(2,1)S(1)} copy-done((bf16[4,1536]{1,0:T(4,128)(2,1)S(1)}, bf16[4,1536]{1,0:T(4,128)(2,1)}, u32[]{:S(2)}) %copy-start.3) | copy-done | bytes 12312
  3.9 0.0 copy-start.4
  3.9 0.7 %copy-done.4 = bf16[32,64]{1,0:T(8,128)(2,1)S(1)} copy-done((bf16[32,64]{1,0:T(8,128)(2,1)S(1)}, bf16[32,64]{1,0:T(8,128)(2,1)}, u32[]{:S(2)}) %copy-start.4) | copy-done | bytes 4120
  4.6 0.0 copy-start.5
  4.6 0.7 %copy-done.5 = f32[16,128]{1,0:T(8,128)S(1)} copy-done((f32[16,128]{1,0:T(8,128)S(1)}, f32[16,128]{1,0:T(8,128)}, u32[]{:S(2)}) %copy-start.5) | copy-done | bytes 8216
  5.3 0.0 copy-start.6
  5.3 0.7 %copy-done.6 = bf16[4,512]{1,0:T(4,128)(2,1)S(1)} copy-done((bf16[4,512]{1,0:T(4,128)(2,1)S(1)}, bf16[4,512]{1,0:T(4,128)(2,1)}, u32[]{:S(2)}) %copy-start.6) | copy-done | bytes 4120
  6.0 0.0 copy-start.7
  6.0 0.7 %copy-done.7 = bf16[4,64]{1,0:T(4,128)(2,1)S(1)} copy-done((bf16[4,64]{1,0:T(4,128)(2,1)S(1)}, bf16[4,64]{1,0:T(4,128)(2,1)}, u32[]{:S(2)}) %copy-start.7) | copy-done | bytes 536
  6.7 0.0 copy-start.8
  6.7 0.7 %copy-done.8 = s32[8]{0:T(128)S(1)} copy-done((s32[8]{0:T(128)S(1)}, s32[8]{0:T(128)}, u32[]{:S(2)}) %copy-start.8) | copy-done | bytes 56
  7.3 44.7 %attention.1 = bf16[64,1024]{1,0:T(8,128)(2,1)S(1)} custom-call(bf16[4,1536]{1,0:T(4,128)(2,1)S(1)} %copy-done.3, bf16[4,512]{1,0:T(4,128)(2,1)S(1)} %copy-done.6, bf16[4,64]{1,0:T(4,128)(2,1)S(1)} %copy-done.7, s32[8]{0:T(128)S(1)} %copy-done.8, bf16[32,512]{1,0:T(8,128)(2,1)S(1)} %copy-done.2, bf16[32,64]{1,0:T(8,128)(2,1)S(1)} %copy-done.4, ...), custom_call_target="tpu_custom_call" | custom-call | tf_op jit(solution)/shard_map/attention/pallas_call | solution.py:365
  52.0 0.7 %copy.12 = bf16[64,1024]{1,0:T(8,128)(2,1)} copy(bf16[64,1024]{1,0:T(8,128)(2,1)S(1)} %attention.1) | data formatting | bytes 262144
Async XLA Ops:
  0.0 1.2 %copy-start = (bf16[8,128,512]{2,1,0:T(8,128)(2,1)S(1)}, bf16[8,128,512]{2,1,0:T(8,128)(2,1)}, u32[]{:S(2)}) copy-start(bf16[8,128,512]{2,1,0:T(8,128)(2,1)} %w_uk.1) | copy-start | bytes 3145732
  1.2 1.2 %copy-start.1 = (bf16[8,512,128]{2,1,0:T(8,128)(2,1)S(1)}, bf16[8,512,128]{2,1,0:T(8,128)(2,1)}, u32[]{:S(2)}) copy-start(bf16[8,512,128]{2,1,0:T(8,128)(2,1)} %w_uv.1) | copy-start | bytes 3145732
  2.5 0.8 %copy-start.2 = (bf16[32,512]{1,0:T(8,128)(2,1)S(1)}, bf16[32,512]{1,0:T(8,128)(2,1)}, u32[]{:S(2)}) copy-start(bf16[32,512]{1,0:T(8,128)(2,1)} %pl_ref.1) | copy-start | bytes 98308
  3.2 0.7 %copy-start.3 = (bf16[4,1536]{1,0:T(4,128)(2,1)S(1)}, bf16[4,1536]{1,0:T(4,128)(2,1)}, u32[]{:S(2)}) copy-start(bf16[4,1536]{1,0:T(4,128)(2,1)} %ql_ref.1) | copy-start | bytes 36868
  3.9 0.7 %copy-start.4 = (bf16[32,64]{1,0:T(8,128)(2,1)S(1)}, bf16[32,64]{1,0:T(8,128)(2,1)}, u32[]{:S(2)}) copy-start(bf16[32,64]{1,0:T(8,128)(2,1)} %pr_ref.1) | copy-start | bytes 12292
  4.6 0.7 %copy-start.5 = (f32[16,128]{1,0:T(8,128)S(1)}, f32[16,128]{1,0:T(8,128)}, u32[]{:S(2)}) copy-start(f32[16,128]{1,0:T(8,128)} %constant.2.clone.table_ref) | copy-start | bytes 24580
  5.3 0.7 %copy-start.6 = (bf16[4,512]{1,0:T(4,128)(2,1)S(1)}, bf16[4,512]{1,0:T(4,128)(2,1)}, u32[]{:S(2)}) copy-start(bf16[4,512]{1,0:T(4,128)(2,1)} %dl_ref.1) | copy-start | bytes 12292
  6.0 0.7 %copy-start.7 = (bf16[4,64]{1,0:T(4,128)(2,1)S(1)}, bf16[4,64]{1,0:T(4,128)(2,1)}, u32[]{:S(2)}) copy-start(bf16[4,64]{1,0:T(4,128)(2,1)} %dr_ref.1) | copy-start | bytes 1540
  6.7 0.7 %copy-start.8 = (s32[8]{0:T(128)S(1)}, s32[8]{0:T(128)}, u32[]{:S(2)}) copy-start(s32[8]{0:T(128)} %start_ref.1) | copy-start | bytes 100

commit v2 on v1

--- a/solution.py
+++ b/solution.py
@@ -70,7 +70,8 @@
 
 
 def kernel(
-    ql_ref, dl_ref, dr_ref, start_ref, pl_ref, pr_ref, table_ref, w_uq, w_uk, w_uv, out_ref,
+    ql_in, dl_in, dr_in, start_in, pl_in, pr_in, table_in, w_uq, w_uk, w_uv, out_ref,
+    ql_ref, dl_ref, dr_ref, start_ref, pl_ref, pr_ref, table_ref,
     keys, q_send, q_all, q_stage, q_own, q_peer, q_full, queries, draft, acc, top, total,
     o_send, o_recv, s_send, s_recv, v_uq, v_uk, v_uv, local_sem, send_sem, recv_sem,
 ):
@@ -98,15 +99,23 @@
     greeted = q_peers + [place(x, (y + 3 + 2 * (y % 2)) % 4, z, core), place(x, (y + 2) % 4, z, core)]
     greeted += [at_z(toward), at_z(3 * toward), at_z(2), at_z(-2), partner, sibling]
 
-    weights = [
+    loads = [
         pltpu.make_async_copy(src, dst, local_sem.at[i])
-        for i, (src, dst) in enumerate(((w_uq, v_uq), (w_uk, v_uk), (w_uv, v_uv)))
+        for i, (src, dst) in enumerate((
+            (pl_in, pl_ref), (pr_in, pr_ref), (ql_in, ql_ref), (dl_in, dl_ref), (dr_in, dr_ref),
+            (table_in, table_ref), (start_in, start_ref), (w_uq, v_uq), (w_uk, v_uk), (w_uv, v_uv),
+        ))
     ]
-    for copy in weights:
+    inputs, weights = loads[:7], loads[7:]
+    for copy in inputs:
         copy.start()
     barrier = pltpu.get_barrier_semaphore()
     for device in greeted:
         pl.semaphore_signal(barrier, inc=1, device_id=device, device_id_type=MESH)
+    for copy in weights:
+        copy.start()
+    for copy in inputs:
+        copy.wait()
 
     sent = []
 
@@ -359,16 +368,22 @@
     q_latent, draft_latent, draft_rope, draft_start, prompt_latent, prompt_rope, w_uq, w_uk, w_uv
 ):
     vmem = pl.BlockSpec(memory_space=pltpu.VMEM)
-    smem = pl.BlockSpec(memory_space=pltpu.SMEM)
-    hbm = pl.BlockSpec(memory_space=pl.ANY)
+    hbm = pl.BlockSpec(memory_space=pltpu.HBM)
     bf16, f32 = jnp.bfloat16, jnp.float32
     return pl.pallas_call(
         kernel,
         name="attention",
         out_shape=jax.ShapeDtypeStruct((ROWS, HEADS * VD), bf16),
-        in_specs=[vmem, vmem, vmem, smem, vmem, vmem, vmem, hbm, hbm, hbm],
+        in_specs=[hbm] * 10,
         out_specs=vmem,
         scratch_shapes=[
+            pltpu.VMEM((4, QLORA), bf16),
+            pltpu.VMEM((4, KVL), bf16),
+            pltpu.VMEM((4, ROPE), bf16),
+            pltpu.SMEM((8,), jnp.int32),
+            pltpu.VMEM((32, KVL), bf16),
+            pltpu.VMEM((32, ROPE), bf16),
+            pltpu.VMEM((16, 128), f32),
             pltpu.VMEM((UNITS * UNIT, 16, 128), bf16),
             pltpu.VMEM((16, 640), bf16),
             pltpu.VMEM((256, 640), bf16),
@@ -388,12 +403,12 @@
             pltpu.VMEM((QLORA, HEADS * (NOPE + ROPE)), bf16),
             pltpu.VMEM((HEADS, NOPE, KVL), bf16),
             pltpu.VMEM((HEADS, KVL, VD), bf16),
-            pltpu.SemaphoreType.DMA((3,)),
+            pltpu.SemaphoreType.DMA((10,)),
             pltpu.SemaphoreType.DMA((80,)),
             pltpu.SemaphoreType.DMA((80,)),
         ],
         compiler_params=pltpu.CompilerParams(
-            collective_id=0, has_side_effects=True, vmem_limit_bytes=48 * 2**20
+            collective_id=0, has_side_effects=True, vmem_limit_bytes=64 * 2**20
         ),
     )(
         q_latent, draft_latent, draft_rope, draft_start, prompt_latent, prompt_rope,

time: 53.1 us -> 46.3 us (0.87)
  local copies, waits for them, and re-layouts: 7.98 us -> 1.57 us
    unnamed x19 -> x1, local copies, waits for them, and re-layouts: 7.98 us -> 1.57 us
where the time goes in v2:
time: 46.3 us; the launch traced here: 46.2 us
  Pallas kernels  44.6 us (96%)
  local copies, waits for them, and re-layouts  1.57 us (3%)
    pallas_call x1, Pallas kernels, on_device(): pl.pallas_call(kernel, name='attention', out_shape=jax.ShapeDtypeStruct((...  44.6 us
    unnamed x1, local copies, waits for them, and re-layouts  1.57 us

profile of v2, /device:TPU:1, one launch (start us, length us, event | category | flops | bytes accessed | tf_op | source)
XLA Modules:
  0.0 46.2 jit_solution(3138070575772687782)
XLA Ops:
  0.0 44.6 %attention.1 = bf16[64,1024]{1,0:T(8,128)(2,1)} custom-call(bf16[4,1536]{1,0:T(4,128)(2,1)} %ql_in.1, bf16[4,512]{1,0:T(4,128)(2,1)} %dl_in.1, bf16[4,64]{1,0:T(4,128)(2,1)} %dr_in.1, s32[8]{0:T(128)} %start_in.1, bf16[32,512]{1,0:T(8,128)(2,1)} %pl_in.1, bf16[32,64]{1,0:T(8,128)(2,1)} %pr_in.1, f32[16,128]{1,0:T(8,128)} %constant.2.clone.table_in, ...), custom_call_target="tpu_custom_call" | custom-call | tf_op jit(solution)/shard_map/attention/pallas_call | solution.py:373
  44.6 1.6 %copy.12 = bf16[64,1024]{1,0:T(8,128)(2,1)} copy(bf16[64,1024]{1,0:T(8,128)(2,1)} %attention.1) | data formatting | bytes 262144

commit v3 on v2

--- a/solution.py
+++ b/solution.py
@@ -37,28 +37,12 @@
     return np.concatenate([cosine, sine], axis=0).astype(np.float32)
 
 
-def early(bs, cs, as_):
-    return (bs * 2 + cs) * 4 + as_
-
-
-def late(bs, cs, as_, zs=0):
-    return 32 + ((bs * 2 + cs) * 4 + as_) * 3 + zs
-
-
-def chunks():
-    both = (0, 1)
-    first = [early(b, c, a) for c in both for b in range(3) for a in range(4)]
-    first += [early(3, c, 0) for c in both] + [late(0, c, 0, z) for c in both for z in range(3)]
-    second = [late(b, c, a, z) for c in both for b, a in ((0, 1), (0, 2), (0, 3), (1, 0), (2, 0)) for z in range(3)]
-    second += [early(3, c, 3) for c in both]
-    third = [late(b, c, 1, z) for c in both for b in (1, 2) for z in range(3)]
-    third += [late(b, c, 2, z) for c in both for b in (1, 2) for z in range(3)]
-    fourth = [late(b, c, 3, z) for c in both for b in (1, 2) for z in range(3)]
-    fourth += [late(3, c, 0, z) for c in both for z in range(3)]
-    fourth += [early(3, c, a) for c in both for a in (1, 2)] + [late(3, c, 1, 0) for c in both]
-    fifth = [late(3, c, 1, z) for c in both for z in (1, 2)]
-    fifth += [late(3, c, a, z) for c in both for a in (2, 3) for z in range(3)]
-    return first, second, third, fourth, fifth
+def unit(stream, bs, cs, as_):
+    return ((stream * 4 + bs) * 2 + cs) * 4 + as_
+
+
+def chunk(streams, bss):
+    return [unit(s, b, c, a) for s in streams for b in bss for c in (0, 1) for a in range(4)]
 
 
 def dot_t(a, b):
@@ -129,16 +113,16 @@
         sent.append(copy)
         return copy
 
-    def tiles(unit, count=1, first=0, last=0):
-        return keys.at[pl.ds(unit * UNIT + first, count * UNIT - first - last)]
+    def tiles(at, count=1, first=0, last=0):
+        return keys.at[pl.ds(at * UNIT + first, count * UNIT - first - last)]
 
     def move(src, dst, count, device, first=0, last=0):
         return send(tiles(src, count, first, last), tiles(dst, count, first, last), device)
 
     for row in range(2):
         for lane in range(4):
-            keys[early(0, 0, 0) * UNIT + row * 4 + lane] = pl_ref[row * 16 : row * 16 + 16, lane * 128 : lane * 128 + 128]
-    keys[early(0, 0, 0) * UNIT + 8] = jnp.concatenate([pr_ref[0:16, :], pr_ref[16:32, :]], axis=1)
+            keys[row * 4 + lane] = pl_ref[row * 16 : row * 16 + 16, lane * 128 : lane * 128 + 128]
+    keys[8] = jnp.concatenate([pr_ref[0:16, :], pr_ref[16:32, :]], axis=1)
     q_stage[...] = jnp.zeros(q_stage.shape, jnp.float32)
     for part in range(4):
         q_stage[part * 4 : part * 4 + 4, 0:384] = ql_ref[:, part * 384 : part * 384 + 384].astype(jnp.float32)
@@ -152,71 +136,69 @@
 
     q_copies = [send(q_send, q_all.at[my_rows, :], device) for device in q_peers]
     z_copies = [
-        move(early(0, 0, 0), late(0, 0, 0, slot), 1, at_z(step))
-        for slot, step in enumerate((toward, -2 * toward, 3 * toward))
+        move(unit(0, 0, 0, 0), unit(stream, 0, 0, 0), 1, at_z(step))
+        for stream, step in ((1, toward), (2, -2 * toward), (3, 3 * toward))
     ]
 
     class Stream:
-        def __init__(self, unit, count):
-            self.unit, self.count = unit, count
-            self.right, self.left, self.far = [None] * 4, [None] * 4, [None] * 8
-            self.side = []
+        def __init__(self, index):
+            self.index = index
+            self.a, self.right, self.left = [None] * 4, [None] * 4, [None] * 4
+            self.far = []
+            self.side = [None] * 4
+
+        def spread(self, k):
+            own = unit(self.index, 0, 0, k)
+            self.right[k] = move(own, unit(self.index, 1, 0, k), 1, at_b(1))
+            self.left[k] = move(own, unit(self.index, 2, 0, k), 1, at_b(-1))
+
+        def to_sibling(self, bs):
+            self.side[bs] = move(unit(self.index, bs, 0, 0), unit(self.index, bs, 1, 0), 4, sibling)
 
         def start(self):
-            unit, count = self.unit, self.count
-            own = unit(0, 0, 0)
-            self.a = [move(own, unit(0, 0, slot), count, at_a(step)) for slot, step in ((1, 1), (2, -1), (3, 2))]
+            if self.index:
+                z_copies[self.index - 1].wait_recv()
+            for k, step in ((1, 1), (2, -1), (3, 2)):
+                self.a[k] = move(unit(self.index, 0, 0, 0), unit(self.index, 0, 0, k), 1, at_a(step))
             self.spread(0)
-            self.to_sibling(0, 0, 1)
-
-        def spread(self, k):
-            unit, count = self.unit, self.count
-            self.right[k] = move(unit(0, 0, k), unit(1, 0, k), count, at_b(1))
-            self.left[k] = move(unit(0, 0, k), unit(2, 0, k), count, at_b(-1))
-
-        def to_sibling(self, bs, k, width):
-            unit, count = self.unit, self.count
-            self.side.append(move(unit(bs, 0, k), unit(bs, 1, k), count * width, sibling))
 
         def arrive_a(self):
             for k in (1, 2, 3):
-                self.a[k - 1].wait_recv()
+                self.a[k].wait_recv()
                 self.spread(k)
-            self.to_sibling(0, 1, 3)
-
-        def arrive_b(self, ks):
-            unit, count = self.unit, self.count
-            cut = count * UNIT // 2
-            for k in ks:
+            self.to_sibling(0)
+
+        def arrive_b(self):
+            cut = UNIT // 2
+            for k in range(4):
+                here = unit(self.index, 3, 0, k)
                 self.right[k].wait_recv()
-                self.far[2 * k] = move(unit(1, 0, k), unit(3, 0, k), count, at_b(1), 0, count * UNIT - cut)
+                self.far.append(move(unit(self.index, 1, 0, k), here, 1, at_b(1), 0, UNIT - cut))
                 self.left[k].wait_recv()
-                self.far[2 * k + 1] = move(unit(2, 0, k), unit(3, 0, k), count, at_b(-1), cut, 0)
-            self.to_sibling(1, ks[0], len(ks))
-            self.to_sibling(2, ks[0], len(ks))
-
-        def arrive_far(self, ks):
-            for k in ks:
-                self.far[2 * k].wait_recv()
-                self.far[2 * k + 1].wait_recv()
-            self.to_sibling(3, ks[0], len(ks))
-
-        def arrive_sibling(self, count):
-            for _ in range(count):
-                self.side.pop(0).wait_recv()
-
-    soon, later = Stream(early, 1), Stream(late, 3)
-    soon.start()
-
-    soon.arrive_a()
-    for copy in z_copies:
-        copy.wait_recv()
-    later.start()
+                self.far.append(move(unit(self.index, 2, 0, k), here, 1, at_b(-1), cut, 0))
+            self.to_sibling(1)
+            self.to_sibling(2)
+
+        def arrive_far(self):
+            for copy in self.far:
+                copy.wait_recv()
+            self.to_sibling(3)
+
+        def arrive_side(self, *bss):
+            for bs in bss:
+                self.side[bs].wait_recv()
+
+    streams = [Stream(i) for i in range(4)]
+    streams[0].start()
+    streams[1].start()
+    streams[0].arrive_a()
+    streams[2].start()
+    streams[3].start()
+
     for copy in q_copies:
         copy.wait_recv()
     half = pl.ds(pl.multiple_of(core * 128, 128), 128)
     q_side = send(q_all.at[half, :], q_all.at[half, :], sibling)
-    soon.arrive_b([0])
     q_side.wait_recv()
 
     row_at = lax.broadcasted_iota(jnp.int32, (ROWS, 256), 0)
@@ -283,15 +265,19 @@
             acc[rows, :] = acc[rows, :] * factor[:, 0:1] + summed
         top[rows, :] = new_top
 
-    def attend(items):
+    def attend(items, done=None):
         held = None
         for group, block, units, first in items:
             rows = pl.ds(group * GROUP + block * BLOCK, BLOCK)
             now = (rows, *score(rows, units), first)
             if held is not None:
                 update(*held)
+                if done is not None:
+                    done(0)
             held = now
         update(*held)
+        if done is not None:
+            done(1)
 
     def attend_draft():
         row = lax.broadcasted_iota(jnp.int32, (BLOCK, ROWS), 0) % ROWS
@@ -311,54 +297,72 @@
         ctx = (acc[rows, :] * (1.0 / total[rows, 0:1])).astype(jnp.bfloat16)
         return dot(ctx, v_uv[h]), top[rows, :] + jnp.log2(total[rows, :])
 
-    c0, c1, c2, c3, c4 = chunks()
+    def pair(group, units, first=False):
+        return [(group, 0, units, first), (group, 1, units, first)]
+
     weights[0].wait()
     weights[1].wait()
     project(0, q_own)
-    soon.arrive_b([1, 2, 3])
+    streams[1].arrive_a()
     attend_draft()
-    soon.arrive_far([0])
-    later.arrive_a()
-    later.arrive_b([0])
-    soon.arrive_far([1, 2, 3])
-    soon.arrive_sibling(8)
-    later.arrive_sibling(1)
-    attend([(0, 0, c0, False), (0, 1, c0, False)])
-    later.arrive_b([1])
+    streams[2].arrive_a()
+    streams[0].arrive_side(0)
+    streams[1].arrive_side(0)
+    attend(pair(0, chunk((0, 1), (0,))))
+    streams[3].arrive_a()
+    streams[0].arrive_b()
     q_peer_copy.wait_recv()
     project(1, q_peer)
-    later.arrive_b([2])
-    later.arrive_sibling(3)
-    attend([(0, 0, c1, False), (0, 1, c1, False)])
-    later.arrive_b([3])
-    later.arrive_far([0])
-    attend([(1, 0, c0, True), (1, 1, c0, True), (1, 0, c1, False), (1, 1, c1, False)])
-    later.arrive_far([1])
-    later.arrive_sibling(4)
-    attend([(1, 0, c2, False), (1, 1, c2, False)])
-    later.arrive_far([2, 3])
-    later.arrive_sibling(4)
-    attend([(1, 0, c3, False), (1, 1, c3, False)])
-    later.arrive_sibling(1)
-    attend([(1, 0, c4, False), (1, 1, c4, False)])
+    streams[1].arrive_b()
+    streams[2].arrive_side(0)
+    streams[3].arrive_side(0)
+    attend(pair(1, chunk((0, 1, 2, 3), (0,)), True))
+    streams[2].arrive_b()
+    streams[3].arrive_b()
+    attend(pair(0, chunk((2, 3), (0,))))
+    streams[0].arrive_side(1, 2)
+    streams[1].arrive_side(1, 2)
+    attend(pair(1, chunk((0, 1), (1, 2))))
+    streams[0].arrive_far()
+    streams[1].arrive_far()
+    streams[2].arrive_side(1, 2)
+    streams[3].arrive_side(1, 2)
+    attend(pair(1, chunk((2, 3), (1, 2))))
+    streams[2].arrive_far()
+    streams[3].arrive_far()
+    streams[0].arrive_side(3)
+    streams[1].arrive_side(3)
+    attend(pair(1, chunk((0, 1), (3,))))
+    streams[2].arrive_side(3)
+    streams[3].arrive_side(3)
     weights[2].wait()
-    shares = jnp.zeros((ROWS, 128), jnp.float32)
-    for h in range(HEADS):
-        value, share = context(1, h)
-        o_send[:, h * VD : h * VD + VD] = value.astype(jnp.bfloat16)
-        shares = jnp.where(lane == h, share, shares)
-    s_send[...] = shares
-    o_copy = send(o_send, o_recv, partner)
-    s_copy = send(s_send, s_recv, partner)
-    attend([(0, b, c, False) for c in (c2, c3, c4) for b in range(2)])
+    o_copies = []
+
+    def hand_over(part):
+        shares = s_send[...] if part else jnp.zeros((ROWS, 128), jnp.float32)
+        for i in range(HEADS // 2):
+            h = part * (HEADS // 2) + i
+            value, share = context(1, h)
+            o_send[part, :, i * VD : i * VD + VD] = value.astype(jnp.bfloat16)
+            shares = jnp.where(lane == h, share, shares)
+        s_send[...] = shares
+        o_copies.append(send(o_send.at[part], o_recv.at[part], partner))
+        if part:
+            o_copies.append(send(s_send, s_recv, partner))
+
+    attend(pair(1, chunk((2, 3), (3,))), hand_over)
+    attend(
+        pair(0, chunk((0, 1), (1, 2))) + pair(0, chunk((2, 3), (1, 2))) + pair(0, chunk((0, 1, 2, 3), (3,)))
+    )
     own = [context(0, h) for h in range(HEADS)]
-    o_copy.wait_recv()
-    s_copy.wait_recv()
+    for copy in o_copies:
+        copy.wait_recv()
     for h, (value, share) in enumerate(own):
         other = jnp.broadcast_to(s_recv[:, h : h + 1], (ROWS, 128))
         mine = 1.0 / (1.0 + jnp.exp2(jnp.minimum(other - share, 120.0)))
         theirs = 1.0 / (1.0 + jnp.exp2(jnp.minimum(share - other, 120.0)))
-        peer = o_recv[:, h * VD : h * VD + VD].astype(jnp.float32)
+        part, at = h // 4, (h % 4) * VD
+        peer = o_recv[part, :, at : at + VD].astype(jnp.float32)
         out_ref[:, h * VD : h * VD + VD] = (value * mine + peer * theirs).astype(jnp.bfloat16)
     for copy in sent:
         copy.wait_send()
@@ -396,16 +400,16 @@
             pltpu.VMEM((2 * GROUP, KVL), f32),
             pltpu.VMEM((2 * GROUP, 128), f32),
             pltpu.VMEM((2 * GROUP, 128), f32),
-            pltpu.VMEM((ROWS, HEADS * VD), bf16),
-            pltpu.VMEM((ROWS, HEADS * VD), bf16),
+            pltpu.VMEM((2, ROWS, HEADS * VD // 2), bf16),
+            pltpu.VMEM((2, ROWS, HEADS * VD // 2), bf16),
             pltpu.VMEM((ROWS, 128), f32),
             pltpu.VMEM((ROWS, 128), f32),
             pltpu.VMEM((QLORA, HEADS * (NOPE + ROPE)), bf16),
             pltpu.VMEM((HEADS, NOPE, KVL), bf16),
             pltpu.VMEM((HEADS, KVL, VD), bf16),
             pltpu.SemaphoreType.DMA((10,)),
-            pltpu.SemaphoreType.DMA((80,)),
-            pltpu.SemaphoreType.DMA((80,)),
+            pltpu.SemaphoreType.DMA((112,)),
+            pltpu.SemaphoreType.DMA((112,)),
         ],
         compiler_params=pltpu.CompilerParams(
             collective_id=0, has_side_effects=True, vmem_limit_bytes=64 * 2**20

time: 46.3 us -> 43 us (0.929)
  Pallas kernels: 44.6 us -> 41.3 us
    pallas_call x1, Pallas kernels: 44.6 us -> 41.3 us  [on_device(): pl.pallas_call(kernel, name='attention', out_shape=jax.ShapeDtypeStruct((...]
where the time goes in v3:
time: 43 us; the launch traced here: 42.9 us
  Pallas kernels  41.3 us (96%)
  local copies, waits for them, and re-layouts  1.57 us (4%)
    pallas_call x1, Pallas kernels, on_device(): pl.pallas_call(kernel, name='attention', out_shape=jax.ShapeDtypeStruct((...  41.3 us
    unnamed x1, local copies, waits for them, and re-layouts  1.57 us

profile of v3, /device:TPU:1, one launch (start us, length us, event | category | flops | bytes accessed | tf_op | source)
XLA Modules:
  0.0 42.9 jit_solution(5271020918208168439)
XLA Ops:
  0.0 41.3 %attention.1 = bf16[64,1024]{1,0:T(8,128)(2,1)} custom-call(bf16[4,1536]{1,0:T(4,128)(2,1)} %ql_in.1, bf16[4,512]{1,0:T(4,128)(2,1)} %dl_in.1, bf16[4,64]{1,0:T(4,128)(2,1)} %dr_in.1, s32[8]{0:T(128)} %start_in.1, bf16[32,512]{1,0:T(8,128)(2,1)} %pl_in.1, bf16[32,64]{1,0:T(8,128)(2,1)} %pr_in.1, f32[16,128]{1,0:T(8,128)} %constant.2.clone.table_in, ...), custom_call_target="tpu_custom_call" | custom-call | tf_op jit(solution)/shard_map/attention/pallas_call | solution.py:377
  41.4 1.6 %copy.12 = bf16[64,1024]{1,0:T(8,128)(2,1)} copy(bf16[64,1024]{1,0:T(8,128)(2,1)} %attention.1) | data formatting | bytes 262144

commit v4 on v3

v4 whole, which is shorter than its diff:
```python
import math

import jax
import jax.numpy as jnp
import numpy as np
from jax import lax
from jax.experimental import pallas as pl
from jax.experimental.pallas import tpu as pltpu
from jax.sharding import PartitionSpec as P

MESH = pl.DeviceIdType.MESH
KVL = 512
ROPE = 64
NOPE = 128
VD = 128
DRAFT = 8
PROMPT = 8192
QLORA = 1536
ROWS = 64
HEADS = 8
GROUP = ROWS * HEADS
SCALE = math.log2(math.e) / math.sqrt(NOPE + ROPE)
UNIT = 9
UNITS = 128
BLOCK = 256
NT = (((1,), (1,)), ((), ()))


def rotation_table():
    half = ROPE // 2
    freq = np.float32(10000.0) ** (-np.arange(half, dtype=np.float32) / np.float32(half))
    position = PROMPT + np.arange(DRAFT, dtype=np.float32)
    angle = (position[:, None] * freq[None, :].astype(np.float32)).astype(np.float64)
    zero = np.zeros((DRAFT, 2 * half))
    cosine = np.concatenate([np.cos(angle), np.cos(angle), zero], axis=1)
    sine = np.concatenate([-np.sin(angle), np.sin(angle), zero], axis=1)
    return np.concatenate([cosine, sine], axis=0).astype(np.float32)


def unit(stream, bs, cs, as_):
    return ((stream * 4 + bs) * 2 + cs) * 4 + as_


def chunk(streams, bss):
    return [unit(s, b, c, a) for s in streams for b in bss for c in (0, 1) for a in range(4)]


def dot_t(a, b):
    return lax.dot_general(a, b, NT, preferred_element_type=jnp.float32)


def dot(a, b):
    return jnp.dot(a, b, preferred_element_type=jnp.float32)


def kernel(
    ql_in, dl_in, dr_in, start_in, pl_in, pr_in, table_in, w_uq, w_uk, w_uv, out_ref,
    ql_ref, dl_ref, dr_ref, start_ref, pl_ref, pr_ref, table_ref,
    keys, q_send, q_all, d_send, d_all, q_stage, q_rows, q_full, queries, draft, draft_bias, acc, top, total,
    o_send, o_recv, s_send, s_recv, shares, v_uq, v_uk, v_uv, local_sem, send_sem, recv_sem,
):
    grp, head = lax.axis_index("grp"), lax.axis_index("head")
    x, y, z, core = head // 4, (grp // 8) * 2 + (head // 2) % 2, grp % 8, head % 2
    toward = 2 * (z % 2) - 1

    def place(px, py, pz, pc):
        return ((py // 2) * 8 + pz, px * 4 + (py % 2) * 2 + pc)

    def at_a(step):
        return place((x + step * core + 4) % 4, (y + step * (1 - core) + 4) % 4, z, core)

    def at_b(step):
        return place((x + step * (1 - core) + 4) % 4, (y + step * core + 4) % 4, z, core)

    def at_z(step):
        return place(x, y, (z + step + 8) % 8, core)

    beside = y + 1 - 2 * (y % 2)
    sibling = place(x, y, z, 1 - core)
    partner = at_z(-toward)
    beyond = (z - toward + 8) % 8
    near = [place((x + dx) % 4, y, z, core) for dx in (1, 3, 2)]
    near += [place((x + dx) % 4, beside, z, core) for dx in (0, 1, 3, 2)]
    across = [place((x + dx) % 4, py, beyond, core) for py in (y, beside) for dx in (0, 1, 3, 2)]
    greeted = near + across + [place(x, (y + 3 + 2 * (y % 2)) % 4, z, core), place(x, (y + 2) % 4, z, core)]
    greeted += [at_z(toward), at_z(3 * toward), at_z(2), at_z(-2), sibling]

    loads = [
        pltpu.make_async_copy(src, dst, local_sem.at[i])
        for i, (src, dst) in enumerate((
            (pl_in, pl_ref), (pr_in, pr_ref), (ql_in, ql_ref), (dl_in, dl_ref), (dr_in, dr_ref),
            (table_in, table_ref), (start_in, start_ref), (w_uq, v_uq), (w_uk, v_uk), (w_uv, v_uv),
        ))
    ]
    inputs, weights = loads[:7], loads[7:]
    for copy in inputs:
        copy.start()
    barrier = pltpu.get_barrier_semaphore()
    for device in greeted:
        pl.semaphore_signal(barrier, inc=1, device_id=device, device_id_type=MESH)
    for copy in weights:
        copy.start()
    for copy in inputs:
        copy.wait()

    def send(src, dst, device, left, landed):
        pltpu.make_async_remote_copy(
            src_ref=src, dst_ref=dst, send_sem=send_sem.at[left], recv_sem=recv_sem.at[landed],
            device_id=device, device_id_type=MESH,
        ).start()

    def arrived(landed, ref):
        pltpu.make_async_copy(ref, ref, recv_sem.at[landed]).wait()

    def gone(left, ref):
        pltpu.make_async_copy(ref, ref, send_sem.at[left]).wait()

    def tiles(at, count=1, first=0, last=0):
        return keys.at[pl.ds(at * UNIT + first, count * UNIT - first - last)]

    def move(src, dst, count, device, landed, first=0, last=0):
        send(tiles(src, count, first, last), tiles(dst, count, first, last), device, 0, landed)

    for row in range(2):
        for lane in range(4):
            keys[row * 4 + lane] = pl_ref[row * 16 : row * 16 + 16, lane * 128 : lane * 128 + 128]
    keys[8] = jnp.concatenate([pr_ref[0:16, :], pr_ref[16:32, :]], axis=1)
    q_stage[...] = jnp.zeros(q_stage.shape, jnp.float32)
    for part in range(4):
        q_stage[part * 4 : part * 4 + 4, 0:384] = ql_ref[:, part * 384 : part * 384 + 384].astype(jnp.float32)
        q_stage[part * 4 : part * 4 + 4, 384:512] = dl_ref[:, part * 128 : part * 128 + 128].astype(jnp.float32)
    q_stage[0:4, 512:576] = dr_ref[...].astype(jnp.float32)
    q_send[...] = q_stage[:, 0:384].astype(jnp.bfloat16)
    d_send[...] = q_stage[:, 384:640].astype(jnp.bfloat16)

    def slot(base):
        return pl.ds(pl.multiple_of(base + head // 2 * 16, 16), 16)

    q_all[slot(core * 256), :] = q_send[...]
    d_all[slot(core * 128), :] = d_send[...]

    pl.semaphore_wait(barrier, len(greeted))

    for device in near:
        send(q_send, q_all.at[slot(core * 256), :], device, 1, 0)
    for device in across:
        send(q_send, q_all.at[slot(core * 256 + 128), :], device, 1, 0)
    for stream, step in ((1, toward), (2, -2 * toward), (3, 3 * toward)):
        move(unit(0, 0, 0, 0), unit(stream, 0, 0, 0), 1, at_z(step), 8 + stream)

    class Stream:
        def __init__(self, index):
            self.index = index
            self.sem = 12 + index * 6

        def spread(self, k):
            own = unit(self.index, 0, 0, k)
            move(own, unit(self.index, 1, 0, k), 1, at_b(1), self.sem + 1)
            move(own, unit(self.index, 2, 0, k), 1, at_b(-1), self.sem + 1)

        def to_sibling(self, bs, count=1):
            sem = self.sem + 3 + (bs + 1) // 2
            for i in range(bs, bs + count):
                move(unit(self.index, i, 0, 0), unit(self.index, i, 1, 0), 4, sibling, sem)

        def start(self):
            if self.index:
                arrived(8 + self.index, tiles(0))
            for k, step in ((1, 1), (2, -1), (3, 2)):
                move(unit(self.index, 0, 0, 0), unit(self.index, 0, 0, k), 1, at_a(step), self.sem)
            self.spread(0)

        def arrive_a(self):
            arrived(self.sem, tiles(0, 3))
            for k in (1, 2, 3):
                self.spread(k)
            self.to_sibling(0)

        def arrive_b(self):
            cut = UNIT // 2
            arrived(self.sem + 1, tiles(0, 8))
            for k in range(4):
                here = unit(self.index, 3, 0, k)
                move(unit(self.index, 1, 0, k), here, 1, at_b(1), self.sem + 2, 0, UNIT - cut)
                move(unit(self.index, 2, 0, k), here, 1, at_b(-1), self.sem + 2, cut, 0)
            self.to_sibling(1, 2)

        def arrive_far(self):
            arrived(self.sem + 2, tiles(0, 4))
            self.to_sibling(3)

        def arrive_side(self, bs):
            arrived(self.sem + 3 + (bs + 1) // 2, tiles(0, 8 if bs == 1 else 4))

    streams = [Stream(i) for i in range(4)]
    streams[0].start()
    streams[1].start()
    for device in near:
        send(d_send, d_all.at[slot(core * 128), :], device, 2, 1)
    streams[0].arrive_a()
    arrived(0, q_all.at[0:240, :])
    q_half = pl.ds(pl.multiple_of(core * 256, 256), 256)
    send(q_all.at[q_half, :], q_all.at[q_half, :], sibling, 3, 2)
    streams[2].start()
    streams[3].start()
    d_half = pl.ds(pl.multiple_of(core * 128, 128), 128)
    arrived(2, q_all.at[0:256, :])

    row_at = lax.broadcasted_iota(jnp.int32, (ROWS, 256), 0)
    col_at = lax.broadcasted_iota(jnp.int32, (ROWS, 256), 1)
    from_head = row_at // 4
    source = ((from_head % 2) * 8 + from_head // 2) * 16 + row_at % 4
    picks = [
        jnp.where(col_at == source + part * 4, 1.0, 0.0).astype(jnp.bfloat16) for part in range(4)
    ]
    for group in range(2):
        mixed = jnp.concatenate([q_all[i + group * 128 : i + group * 128 + 128, :] for i in (0, 256)], axis=0)
        for part in range(4):
            q_rows[group * ROWS : group * ROWS + ROWS, part * 384 : part * 384 + 384] = dot(
                picks[part], mixed
            ).astype(jnp.bfloat16)

    lane = lax.broadcasted_iota(jnp.int32, (ROWS, 128), 1)
    wide = lax.broadcasted_iota(jnp.int32, (2 * ROWS, 128), 1)

    def project():
        q_full[...] = dot(q_rows[...], v_uq[...]).astype(jnp.bfloat16).astype(jnp.float32)

    def absorb_all():
        cosine = jnp.concatenate([table_ref[0:8, :]] * 16, axis=0)
        sine = jnp.concatenate([table_ref[8:16, :]] * 16, axis=0)

        def absorb(h, nope, pe):
            turned = jnp.where(wide < 32, pltpu.roll(pe, 96, 1), pltpu.roll(pe, 32, 1))
            rotated = pe * cosine + turned * sine
            first = rotated.astype(jnp.bfloat16)
            second = pltpu.roll(rotated, 64, 1).astype(jnp.bfloat16)
            absorbed = dot(nope.astype(jnp.bfloat16), v_uk[h]).astype(jnp.bfloat16)
            for group in range(2):
                rows = pl.ds(group * GROUP + h * ROWS, ROWS)
                part = slice(group * ROWS, group * ROWS + ROWS)
                queries[rows, 0:128] = first[part]
                queries[rows, 640:768] = second[part]
                queries[rows, 128:640] = absorbed[part]

        for two in range(HEADS // 2):
            at = two * 384
            middle = q_full[:, at + 128 : at + 256]
            end = pltpu.roll(q_full[:, at + 256 : at + 384], 64, 1)
            absorb(2 * two, q_full[:, at : at + 128], middle)
            absorb(2 * two + 1, jnp.where(wide < 64, pltpu.roll(middle, 64, 1), end), end)

    def score(rows, units, with_draft=False):
        low = [jnp.concatenate([keys[u * UNIT + t] for u in units], axis=0) for t in range(4)]
        high = [jnp.concatenate([keys[u * UNIT + 4 + t] for u in units], axis=0) for t in range(4)]
        rope = jnp.concatenate([keys[u * UNIT + 8] for u in units], axis=0)
        left = dot_t(queries[rows, 0:640], jnp.concatenate([rope] + low, axis=1))
        right = dot_t(queries[rows, 128:768], jnp.concatenate(high + [rope], axis=1))
        values = [jnp.concatenate(low, axis=1), jnp.concatenate(high, axis=1)]
        scores = [left * SCALE, right * SCALE]
        if with_draft:
            bias = jnp.concatenate([draft_bias[...]] * (BLOCK // ROWS), axis=0)
            scores.append(dot_t(queries[rows, 0:640], draft[...]) * SCALE + bias)
            values.append(draft[:, 128:640])
        return jnp.concatenate(scores, axis=1), jnp.concatenate(values, axis=0)

    def update(rows, scores, values, first=False):
        peak = jnp.max(scores, axis=1, keepdims=True)
        if first:
            new_top = jnp.broadcast_to(peak, (BLOCK, 128))
        else:
            old_top = top[rows, :]
            new_top = jnp.maximum(old_top, peak)
            factor = jnp.exp2(old_top - new_top)
        e = jnp.exp2(scores - new_top[:, 0:1])
        part = jnp.sum(e, axis=1, keepdims=True)
        summed = dot(e.astype(jnp.bfloat16), values)
        if first:
            total[rows, :] = jnp.broadcast_to(part, (BLOCK, 128))
            acc[rows, :] = summed
        else:
            total[rows, :] = total[rows, :] * factor + part
            acc[rows, :] = acc[rows, :] * factor[:, 0:1] + summed
        top[rows, :] = new_top

    held = []

    def settle():
        if held:
            update(*held.pop())

    def attend(items):
        for group, block, units, first, with_draft in items:
            rows = pl.ds(group * GROUP + block * BLOCK, BLOCK)
            now = (rows, *score(rows, units, with_draft), first)
            settle()
            held.append(now)

    def gather_draft():
        draft[ROWS:128, :] = jnp.zeros((128 - ROWS, 640), jnp.bfloat16)
        for part in range(4):
            picked = dot(picks[part], d_all[...]).astype(jnp.bfloat16)
            draft[0:ROWS, 128 + part * 128 : 256 + part * 128] = picked[:, 0:128]
            if part == 0:
                draft[0:ROWS, 0:128] = picked[:, 128:256]
        row = lax.broadcasted_iota(jnp.int32, (ROWS, 128), 0)
        col = lax.broadcasted_iota(jnp.int32, (ROWS, 128), 1)
        begin = jnp.zeros((ROWS, 128), jnp.int32)
        for i in range(8):
            begin = jnp.where((col >> 3) == i, start_ref[i], begin)
        seen = ((row >> 3) == (col >> 3)) & (col <= row) & (begin <= (col & 7))
        draft_bias[...] = jnp.where(seen, 0.0, -1e30)

    def context(group, h):
        rows = pl.ds(group * GROUP + h * ROWS, ROWS)
        ctx = (acc[rows, :] * (1.0 / total[rows, 0:1])).astype(jnp.bfloat16)
        return dot(ctx, v_uv[h]), top[rows, :] + jnp.log2(total[rows, :])

    def pair(group, units, first=False, with_draft=False):
        return [(group, block, units, first, with_draft) for block in range(2)]

    weights[0].wait()
    weights[1].wait()
    project()
    streams[1].arrive_a()
    absorb_all()
    streams[0].arrive_side(0)
    streams[1].arrive_side(0)
    attend(pair(1, chunk((0, 1), (0,)), True))
    streams[2].arrive_a()
    arrived(1, d_all.at[0:112, :])
    send(d_all.at[d_half, :], d_all.at[d_half, :], sibling, 4, 3)
    attend(pair(0, chunk((0, 1), (0,)), True))
    streams[3].arrive_a()
    streams[0].arrive_b()
    streams[2].arrive_side(0)
    streams[3].arrive_side(0)
    attend(pair(1, chunk((2, 3), (0,))))
    streams[1].arrive_b()
    attend(pair(0, chunk((2, 3), (0,))))
    streams[2].arrive_b()
    streams[0].arrive_side(1)
    streams[1].arrive_side(1)
    attend(pair(1, chunk((0, 1), (1, 2))))
    streams[3].arrive_b()
    arrived(3, d_all.at[0:128, :])
    gather_draft()
    attend(pair(0, chunk((0, 1), (1, 2))))
    streams[0].arrive_far()
    streams[1].arrive_far()
    streams[2].arrive_side(1)
    streams[3].arrive_side(1)
    attend(pair(1, chunk((2, 3), (1, 2))))
    streams[2].arrive_far()
    streams[3].arrive_far()
    streams[0].arrive_side(3)
    streams[1].arrive_side(3)
    attend(pair(1, chunk((0, 1), (3,))))
    streams[2].arrive_side(3)
    streams[3].arrive_side(3)
    weights[2].wait()
    def hand_over(part):
        if part == 0:
            shares[...] = jnp.zeros((128, 128), jnp.float32)
        for i in range(HEADS // 2):
            h = part * (HEADS // 2) + i
            value, share = context(1, h)
            o_send[part, :, i * VD : i * VD + VD] = value.astype(jnp.bfloat16)
            shares[0:ROWS, :] = jnp.where(lane == h, share, shares[0:ROWS, :])
        send(o_send.at[part], o_recv.at[part], partner, 5, 4)
        if part:
            s_send[...] = jnp.transpose(shares[...])[0:HEADS, :]
            send(s_send, s_recv, partner, 6, 5)

    attend(pair(1, chunk((2, 3), (3,))))
    hand_over(0)
    rest = pair(0, chunk((2, 3), (1, 2)), False, True) + pair(0, chunk((0, 1, 2, 3), (3,)))
    attend(rest[:1])
    hand_over(1)
    attend(rest[1:])
    settle()
    own = []

    def finish():
        own.extend(context(0, h) for h in range(HEADS))

    def collect():
        arrived(4, o_recv)
        arrived(5, s_recv)

    def merge():
        shares[0:HEADS, :] = s_recv[...]
        others = jnp.transpose(shares[...])
        for h, (value, share) in enumerate(own):
            other = jnp.broadcast_to(others[0:ROWS, h : h + 1], (ROWS, 128))
            mine = 1.0 / (1.0 + jnp.exp2(jnp.minimum(other - share, 120.0)))
            theirs = 1.0 / (1.0 + jnp.exp2(jnp.minimum(share - other, 120.0)))
            part, at = h // 4, (h % 4) * VD
            peer = o_recv[part, :, at : at + VD].astype(jnp.float32)
            out_ref[:, h * VD : h * VD + VD] = (value * mine + peer * theirs).astype(jnp.bfloat16)

    def drain():
        gone(0, tiles(0, 127))
        gone(1, q_all.at[0:240, :])
        gone(2, d_all.at[0:112, :])
        gone(3, q_all.at[0:256, :])
        gone(4, d_all.at[0:128, :])
        gone(5, o_send)
        gone(6, s_send)

    finish()
    collect()
    merge()
    drain()


def on_device(
    q_latent, draft_latent, draft_rope, draft_start, prompt_latent, prompt_rope, w_uq, w_uk, w_uv
):
    vmem = pl.BlockSpec(memory_space=pltpu.VMEM)
    hbm = pl.BlockSpec(memory_space=pltpu.HBM)
    bf16, f32 = jnp.bfloat16, jnp.float32
    return pl.pallas_call(
        kernel,
        name="attention",
        out_shape=jax.ShapeDtypeStruct((ROWS, HEADS * VD), bf16),
        in_specs=[hbm] * 10,
        out_specs=vmem,
        scratch_shapes=[
            pltpu.VMEM((4, QLORA), bf16),
            pltpu.VMEM((4, KVL), bf16),
            pltpu.VMEM((4, ROPE), bf16),
            pltpu.SMEM((8,), jnp.int32),
            pltpu.VMEM((32, KVL), bf16),
            pltpu.VMEM((32, ROPE), bf16),
            pltpu.VMEM((16, 128), f32),
            pltpu.VMEM((UNITS * UNIT, 16, 128), bf16),
            pltpu.VMEM((16, 384), bf16),
            pltpu.VMEM((512, 384), bf16),
            pltpu.VMEM((16, 256), bf16),
            pltpu.VMEM((256, 256), bf16),
            pltpu.VMEM((16, 640), f32),
            pltpu.VMEM((2 * ROWS, QLORA), bf16),
            pltpu.VMEM((2 * ROWS, QLORA), f32),
            pltpu.VMEM((2 * GROUP, 768), bf16),
            pltpu.VMEM((128, 640), bf16),
            pltpu.VMEM((ROWS, 128), f32),
            pltpu.VMEM((2 * GROUP, KVL), f32),
            pltpu.VMEM((2 * GROUP, 128), f32),
            pltpu.VMEM((2 * GROUP, 128), f32),
            pltpu.VMEM((2, ROWS, HEADS * VD // 2), bf16),
            pltpu.VMEM((2, ROWS, HEADS * VD // 2), bf16),
            pltpu.VMEM((HEADS, 128), f32),
            pltpu.VMEM((HEADS, 128), f32),
            pltpu.VMEM((128, 128), f32),
            pltpu.VMEM((QLORA, HEADS * (NOPE + ROPE)), bf16),
            pltpu.VMEM((HEADS, NOPE, KVL), bf16),
            pltpu.VMEM((HEADS, KVL, VD), bf16),
            pltpu.SemaphoreType.DMA((10,)),
            pltpu.SemaphoreType.DMA((7,)),
            pltpu.SemaphoreType.DMA((36,)),
        ],
        compiler_params=pltpu.CompilerParams(
            collective_id=0, has_side_effects=True, vmem_limit_bytes=64 * 2**20
        ),
    )(
        q_latent, draft_latent, draft_rope, draft_start, prompt_latent, prompt_rope,
        rotation_table(), w_uq, w_uk, w_uv,
    )


def solution(mesh):
    in_specs = (
        P(("grp", "head"), None),
        P(("grp", "head"), None),
        P(("grp", "head"), None),
        P("grp"),
        P(("grp", "head"), None),
        P(("grp", "head"), None),
        P(None, "head"),
        P("head", None, None),
        P("head", None, None),
    )
    out_specs = P("grp", "head")
    return jax.shard_map(
        on_device, mesh=mesh, in_specs=in_specs, out_specs=out_specs, check_vma=False
    )
```

time: 43 us -> 41.5 us (0.965)
  Pallas kernels: 41.3 us -> 39.8 us
    pallas_call x1, Pallas kernels: 41.3 us -> 39.8 us  [on_device(): pl.pallas_call(kernel, name='attention', out_shape=jax.ShapeDtypeStruct((...]
where the time goes in v4:
time: 41.5 us; the launch traced here: 41.4 us
  Pallas kernels  39.8 us (96%)
  local copies, waits for them, and re-layouts  1.57 us (4%)
    pallas_call x1, Pallas kernels, on_device(): pl.pallas_call(kernel, name='attention', out_shape=jax.ShapeDtypeStruct((...  39.8 us
    unnamed x1, local copies, waits for them, and re-layouts  1.57 us

profile of v4, /device:TPU:1, one launch (start us, length us, event | category | flops | bytes accessed | tf_op | source)
XLA Modules:
  0.0 41.4 jit_solution(5303373013636250988)
XLA Ops:
  0.0 39.8 %attention.1 = bf16[64,1024]{1,0:T(8,128)(2,1)} custom-call(bf16[4,1536]{1,0:T(4,128)(2,1)} %ql_in.1, bf16[4,512]{1,0:T(4,128)(2,1)} %dl_in.1, bf16[4,64]{1,0:T(4,128)(2,1)} %dr_in.1, s32[8]{0:T(128)} %start_in.1, bf16[32,512]{1,0:T(8,128)(2,1)} %pl_in.1, bf16[32,64]{1,0:T(8,128)(2,1)} %pr_in.1, f32[16,128]{1,0:T(8,128)} %constant.2.clone.table_in, ...), custom_call_target="tpu_custom_call" | custom-call | tf_op jit(solution)/shard_map/attention/pallas_call | solution.py:423
  39.8 1.6 %copy.12 = bf16[64,1024]{1,0:T(8,128)(2,1)} copy(bf16[64,1024]{1,0:T(8,128)(2,1)} %attention.1) | data formatting | bytes 262144

commit v5 on v4

--- a/solution.py
+++ b/solution.py
@@ -85,6 +85,9 @@
     greeted = near + across + [place(x, (y + 3 + 2 * (y % 2)) % 4, z, core), place(x, (y + 2) % 4, z, core)]
     greeted += [at_z(toward), at_z(3 * toward), at_z(2), at_z(-2), sibling]
 
+    barrier = pltpu.get_barrier_semaphore()
+    for device in greeted:
+        pl.semaphore_signal(barrier, inc=1, device_id=device, device_id_type=MESH)
     loads = [
         pltpu.make_async_copy(src, dst, local_sem.at[i])
         for i, (src, dst) in enumerate((
@@ -95,9 +98,6 @@
     inputs, weights = loads[:7], loads[7:]
     for copy in inputs:
         copy.start()
-    barrier = pltpu.get_barrier_semaphore()
-    for device in greeted:
-        pl.semaphore_signal(barrier, inc=1, device_id=device, device_id_type=MESH)
     for copy in weights:
         copy.start()
     for copy in inputs:
@@ -204,21 +204,23 @@
     streams[2].start()
     streams[3].start()
     d_half = pl.ds(pl.multiple_of(core * 128, 128), 128)
+
+    row_at = lax.broadcasted_iota(jnp.int32, (256, 256), 0)
+    col_at = lax.broadcasted_iota(jnp.int32, (256, 256), 1)
+    from_head = (row_at >> 2) & 15
+    source = ((from_head & 1) * 8 + (from_head >> 1)) * 16 + (row_at >> 6) * 4 + (row_at & 3)
+    picks = jnp.where(col_at == source, 1.0, 0.0).astype(jnp.bfloat16)
     arrived(2, q_all.at[0:256, :])
-
-    row_at = lax.broadcasted_iota(jnp.int32, (ROWS, 256), 0)
-    col_at = lax.broadcasted_iota(jnp.int32, (ROWS, 256), 1)
-    from_head = row_at // 4
-    source = ((from_head % 2) * 8 + from_head // 2) * 16 + row_at % 4
-    picks = [
-        jnp.where(col_at == source + part * 4, 1.0, 0.0).astype(jnp.bfloat16) for part in range(4)
+    mixed = [
+        jnp.concatenate([q_all[i + group * 128 : i + group * 128 + 128, :] for i in (0, 256)], axis=0)
+        for group in range(2)
     ]
+    picked = dot(picks, jnp.concatenate(mixed, axis=1)).astype(jnp.bfloat16)
     for group in range(2):
-        mixed = jnp.concatenate([q_all[i + group * 128 : i + group * 128 + 128, :] for i in (0, 256)], axis=0)
         for part in range(4):
-            q_rows[group * ROWS : group * ROWS + ROWS, part * 384 : part * 384 + 384] = dot(
-                picks[part], mixed
-            ).astype(jnp.bfloat16)
+            q_rows[group * ROWS : group * ROWS + ROWS, part * 384 : part * 384 + 384] = picked[
+                part * ROWS : part * ROWS + ROWS, group * 384 : group * 384 + 384
+            ]
 
     lane = lax.broadcasted_iota(jnp.int32, (ROWS, 128), 1)
     wide = lax.broadcasted_iota(jnp.int32, (2 * ROWS, 128), 1)
@@ -298,11 +300,10 @@
 
     def gather_draft():
         draft[ROWS:128, :] = jnp.zeros((128 - ROWS, 640), jnp.bfloat16)
+        chosen = dot(picks, d_all[...]).astype(jnp.bfloat16)
+        draft[0:ROWS, 0:128] = chosen[0:ROWS, 128:256]
         for part in range(4):
-            picked = dot(picks[part], d_all[...]).astype(jnp.bfloat16)
-            draft[0:ROWS, 128 + part * 128 : 256 + part * 128] = picked[:, 0:128]
-            if part == 0:
-                draft[0:ROWS, 0:128] = picked[:, 128:256]
+            draft[0:ROWS, 128 + part * 128 : 256 + part * 128] = chosen[part * ROWS : part * ROWS + ROWS, 0:128]
         row = lax.broadcasted_iota(jnp.int32, (ROWS, 128), 0)
         col = lax.broadcasted_iota(jnp.int32, (ROWS, 128), 1)
         begin = jnp.zeros((ROWS, 128), jnp.int32)
@@ -330,9 +331,13 @@
     streams[2].arrive_a()
     arrived(1, d_all.at[0:112, :])
     send(d_all.at[d_half, :], d_all.at[d_half, :], sibling, 4, 3)
-    attend(pair(0, chunk((0, 1), (0,)), True))
+    own_early = pair(0, chunk((0, 1), (0,)), True)
+    attend(own_early[:1])
     streams[3].arrive_a()
     streams[0].arrive_b()
+    attend(own_early[1:])
+    arrived(3, d_all.at[0:128, :])
+    gather_draft()
     streams[2].arrive_side(0)
     streams[3].arrive_side(0)
     attend(pair(1, chunk((2, 3), (0,))))
@@ -341,10 +346,10 @@
     streams[2].arrive_b()
     streams[0].arrive_side(1)
     streams[1].arrive_side(1)
-    attend(pair(1, chunk((0, 1), (1, 2))))
+    peer_middle = pair(1, chunk((0, 1), (1, 2)))
+    attend(peer_middle[:1])
     streams[3].arrive_b()
-    arrived(3, d_all.at[0:128, :])
-    gather_draft()
+    attend(peer_middle[1:])
     attend(pair(0, chunk((0, 1), (1, 2))))
     streams[0].arrive_far()
     streams[1].arrive_far()
@@ -375,9 +380,9 @@
     attend(pair(1, chunk((2, 3), (3,))))
     hand_over(0)
     rest = pair(0, chunk((2, 3), (1, 2)), False, True) + pair(0, chunk((0, 1, 2, 3), (3,)))
-    attend(rest[:1])
+    settle()
     hand_over(1)
-    attend(rest[1:])
+    attend(rest)
     settle()
     own = []
 

time: 41.5 us -> 41.1 us (level)
  no operation moved by 1% of the time
where the time goes in v5:
time: 41.1 us; the launch traced here: 41 us
  Pallas kernels  39.4 us (96%)
  local copies, waits for them, and re-layouts  1.57 us (4%)
    pallas_call x1, Pallas kernels, on_device(): pl.pallas_call(kernel, name='attention', out_shape=jax.ShapeDtypeStruct((...  39.4 us
    unnamed x1, local copies, waits for them, and re-layouts  1.57 us

profile of v5, /device:TPU:1, one launch (start us, length us, event | category | flops | bytes accessed | tf_op | source)
XLA Modules:
  0.0 41.0 jit_solution(9745040606515852945)
XLA Ops:
  0.0 39.4 %attention.1 = bf16[64,1024]{1,0:T(8,128)(2,1)} custom-call(bf16[4,1536]{1,0:T(4,128)(2,1)} %ql_in.1, bf16[4,512]{1,0:T(4,128)(2,1)} %dl_in.1, bf16[4,64]{1,0:T(4,128)(2,1)} %dr_in.1, s32[8]{0:T(128)} %start_in.1, bf16[32,512]{1,0:T(8,128)(2,1)} %pl_in.1, bf16[32,64]{1,0:T(8,128)(2,1)} %pr_in.1, f32[16,128]{1,0:T(8,128)} %constant.2.clone.table_in, ...), custom_call_target="tpu_custom_call" | custom-call | tf_op jit(solution)/shard_map/attention/pallas_call | solution.py:428
  39.4 1.6 %copy.12 = bf16[64,1024]{1,0:T(8,128)(2,1)} copy(bf16[64,1024]{1,0:T(8,128)(2,1)} %attention.1) | data formatting | bytes 262144

commit v6 on v5

--- a/solution.py
+++ b/solution.py
@@ -355,8 +355,10 @@
     streams[1].arrive_far()
     streams[2].arrive_side(1)
     streams[3].arrive_side(1)
-    attend(pair(1, chunk((2, 3), (1, 2))))
+    peer_late = pair(1, chunk((2, 3), (1, 2)))
+    attend(peer_late[:1])
     streams[2].arrive_far()
+    attend(peer_late[1:])
     streams[3].arrive_far()
     streams[0].arrive_side(3)
     streams[1].arrive_side(3)

time: 41.1 us -> 41 us (level)
  no operation moved by 1% of the time
where the time goes in v6:
time: 41 us; the launch traced here: 40.9 us
  Pallas kernels  39.3 us (96%)
  local copies, waits for them, and re-layouts  1.57 us (4%)
    pallas_call x1, Pallas kernels, on_device(): pl.pallas_call(kernel, name='attention', out_shape=jax.ShapeDtypeStruct((...  39.3 us
    unnamed x1, local copies, waits for them, and re-layouts  1.57 us

profile of v6, /device:TPU:1, one launch (start us, length us, event | category | flops | bytes accessed | tf_op | source)
XLA Modules:
  0.0 40.9 jit_solution(973284853797440490)
XLA Ops:
  0.0 39.3 %attention.1 = bf16[64,1024]{1,0:T(8,128)(2,1)} custom-call(bf16[4,1536]{1,0:T(4,128)(2,1)} %ql_in.1, bf16[4,512]{1,0:T(4,128)(2,1)} %dl_in.1, bf16[4,64]{1,0:T(4,128)(2,1)} %dr_in.1, s32[8]{0:T(128)} %start_in.1, bf16[32,512]{1,0:T(8,128)(2,1)} %pl_in.1, bf16[32,64]{1,0:T(8,128)(2,1)} %pr_in.1, f32[16,128]{1,0:T(8,128)} %constant.2.clone.table_in, ...), custom_call_target="tpu_custom_call" | custom-call | tf_op jit(solution)/shard_map/attention/pallas_call | solution.py:430
  39.3 1.6 %copy.12 = bf16[64,1024]{1,0:T(8,128)(2,1)} copy(bf16[64,1024]{1,0:T(8,128)(2,1)} %attention.1) | data formatting | bytes 262144
